TPU v7x, 256 devices: a whole 4x4x8 slice. The times are simulated.
256 devices in a mesh: own: 8 (over z), col: 8 (over x, core), mlp: 4 (over y).
Axes of the slice: x: 4, y: 4, z: 8, core: 2. Of those that a mesh axis runs over, the one named last changes fastest.
Arguments:
- features: bfloat16 [262144, 512], P(('own', 'col')), may hold values from -6 to 6
- nbr_page: int32 [8192, 32], P(('own', 'col')), may hold values from 0 to 262143, as said below
- nbr_weight: bfloat16 [8192, 32], P(('own', 'col')), may hold values from 0.0049743652 to 0.29882812
- labels: int32 [8192], P(('own', 'col')), may hold values from 0 to 255
- w_one: bfloat16 [512, 2048], P(None, 'mlp'), may hold values from -0.25 to 0.25
- w_two: bfloat16 [2048, 256], P('mlp'), may hold values from -0.125 to 0.125
Outputs:
- grad_one: float32 [512, 2048], P(None, 'mlp')
- grad_two: float32 [2048, 256], P('mlp')
Inputs may be any that keep to these rules, and one draw needn't show every extreme that they name: `nbr_page`: page p is held by owner p // 4096 (owners numbered along own then col) at its row p % 4096. The 32 neighbours of a target are distinct pages listed in non-decreasing order of owner. Of the 4096 neighbour entries of the targets of one index of own and col, at most 128 fall on one owner; one owner receives exactly 128 entries from every index, and some owners receive none from some indices.
All inputs are finite; a program needn't handle non-finite values.
Results may differ from a plain program's by a relative error of at most 0.011.
Values may be sent and summed in bfloat16 or wider, within the bound.
No kernel may reach another device: no remote copies, remote signals or barrier semaphores. Data moves between devices by JAX's collectives and lax.ppermute only.
A program may use at most 128 MiB of HBM per device.

v0:
```python
import jax
import jax.numpy as jnp
from jax import lax
from jax.sharding import PartitionSpec as P


def body(features, nbr_page, nbr_weight, labels, w_one, w_two):
    rows_dev = features.shape[0]
    width_f = features.shape[1]
    targets = nbr_page.shape[0]
    width_k = nbr_page.shape[1]
    owners = lax.axis_size(("own", "col"))
    entries = targets * width_k
    capacity = 2 * entries // owners
    owner_ids = nbr_page // rows_dev
    local_row = nbr_page % rows_dev
    owner_range = jnp.arange(owners, dtype=jnp.int32)
    matches = (owner_ids[:, :, None] == owner_range[None, None, :]).astype(jnp.int32)
    row_count = jnp.sum(matches, axis=1)
    earlier_rows = jnp.cumsum(row_count, axis=0) - row_count
    before_owner = jnp.cumsum(row_count, axis=1) - row_count
    first_slot = earlier_rows - before_owner + owner_range[None, :] * capacity
    slot_ids = (
        jnp.sum(matches * first_slot[:, None, :], axis=2)
        + jnp.arange(width_k, dtype=jnp.int32)[None, :]
    )
    flat_slot = slot_ids.reshape(-1)
    requests = jnp.zeros((owners * capacity,), jnp.int32).at[flat_slot].set(local_row.reshape(-1))
    requests = requests.reshape(owners, capacity)
    asked_rows = lax.all_to_all(requests, ("own", "col"), split_axis=0, concat_axis=0, tiled=True)
    fetched = features[asked_rows]
    returned = lax.all_to_all(fetched, ("own", "col"), split_axis=0, concat_axis=0, tiled=True)
    received = returned.reshape(owners * capacity, width_f)
    contract_first = (((0,), (0,)), ((), ()))
    target_ids = jnp.broadcast_to(
        jnp.arange(targets, dtype=jnp.int32)[:, None], (targets, width_k)
    ).reshape(-1)
    spread = (
        jnp.zeros((targets, owners * capacity), jnp.bfloat16)
        .at[target_ids, flat_slot]
        .set(nbr_weight.reshape(-1))
    )
    pre_act = jnp.dot(received, w_one, preferred_element_type=jnp.float32)
    active = jnp.maximum(pre_act, 0.0).astype(jnp.bfloat16)
    hidden = jnp.dot(spread, active, preferred_element_type=jnp.float32).astype(jnp.bfloat16)
    partial_logits = jnp.dot(hidden, w_two, preferred_element_type=jnp.float32)
    logits = lax.psum(partial_logits, "mlp")
    exponent = jnp.exp(logits)
    probability = exponent / jnp.sum(exponent, axis=1, keepdims=True)
    classes = w_two.shape[1]
    onehot_label = (labels[:, None] == jnp.arange(classes, dtype=jnp.int32)[None, :]).astype(
        jnp.float32
    )
    d_logits = (probability - onehot_label).astype(jnp.bfloat16)
    grad_two = lax.dot_general(hidden, d_logits, contract_first, preferred_element_type=jnp.float32)
    d_hidden = lax.dot_general(
        d_logits, w_two, (((1,), (1,)), ((), ())), preferred_element_type=jnp.float32
    ).astype(jnp.bfloat16)
    positive = (pre_act > 0).astype(jnp.float32)
    scattered = lax.dot_general(
        spread, d_hidden, contract_first, preferred_element_type=jnp.float32
    )
    d_pre = (scattered * positive).astype(jnp.bfloat16)
    grad_one = lax.dot_general(received, d_pre, contract_first, preferred_element_type=jnp.float32)
    grad_one, grad_two = lax.psum((grad_one, grad_two), ("own", "col"))
    return (grad_one, grad_two)


def solution(mesh):
    placed = (
        P(("own", "col"), None),
        P(("own", "col"), None),
        P(("own", "col"), None),
        P(("own", "col")),
        P(None, "mlp"),
        P("mlp", None),
    )
    return jax.shard_map(
        body,
        mesh=mesh,
        in_specs=placed,
        out_specs=(P(None, "mlp"), P("mlp", None)),
        check_vma=False,
    )
```

profile of v0, /device:TPU:8, one launch (start us, length us, event | category | flops | bytes accessed | tf_op | source)
XLA Modules:
  0.0 551.1 jit_solution(711926448814235918)
XLA Ops:
  7.2 0.8 add_select_fusion
  8.6 0.2 reduce_window_sum.22
  8.8 0.2 select_reduce_fusion
  9.4 15.5 %scatter_custom_fusion = s32[8192]{0:T(1024)S(1)} fusion(s32[4096]{0:T(1024)S(1)} %bitcast.22, s32[4096]{0:T(1024)S(1)} %reshape.163, s32[]{:T(128)} %constant.41.clone.1), kind=kCustom, calls=%fused_computation.34 | custom fusion | bytes 32772 | tf_op jit(solution)/shard_map/scatter | solution.py:28
  25.0 21.3 %all_to_all.17 = s32[64,1,128]{2,1,0:T(1,128)S(1)} all-to-all(s32[64,1,128]{2,1,0:T(1,128)S(1)} %bitcast.23), channel_id=1, replica_groups=mesh['own'=8,'col'=8,'mlp'=4] {'own','col'}, dimensions={0} | all-to-all | bytes 65536 | tf_op jit(solution)/shard_map/all_to_all | solution.py:30
  46.3 36.5 %gather_fusion = bf16[8192,512]{1,0:T(8,128)(2,1)} fusion(bf16[4096,512]{1,0:T(8,128)(2,1)} %param.6, s32[8192]{0:T(1024)S(1)} %fusion.7), kind=kCustom, calls=%fused_computation | custom fusion | bytes 16809984 | tf_op jit(solution)/shard_map/gather | solution.py:31
  82.8 5.9 %all-to-all-start.1 = ((bf16[64,128,512]{2,1,0:T(8,128)(2,1)}), bf16[64,128,512]{2,1,0:T(8,128)(2,1)}, u32[]{:S(2)}, u32[]{:S(2)}) async-start(bf16[64,128,512]{2,1,0:T(8,128)(2,1)} %bitcast.21), calls=%async_computation.1 | async-start | bytes 16777216 | tf_op jit(solution)/shard_map/all_to_all | solution.py:32
  88.8 0.1 copy.23
  89.1 0.1 and_reduce_fusion
  89.3 30.4 %scatter_custom_fusion.1 = bf16[1048576]{0:T(1024)(128)(2,1)} fusion(s32[4096]{0:T(1024)S(1)} %broadcast_select_fusion, bf16[4096]{0:T(1024)(128)(2,1)S(1)} %reshape.169, bf16[]{:T(256)} %constant.50.clone.1), kind=kCustom, calls=%fused_computation.10 | custom fusion | bytes 2097154
  119.7 2.8 reshape.150
  122.5 152.3 %all-to-all-done.1 = bf16[64,128,512]{2,1,0:T(8,128)(2,1)} async-done(((bf16[64,128,512]{2,1,0:T(8,128)(2,1)}), bf16[64,128,512]{2,1,0:T(8,128)(2,1)}, u32[]{:S(2)}, u32[]{:S(2)}) %all-to-all-start.1) | async-done | bytes 8388640 | tf_op jit(solution)/shard_map/all_to_all | solution.py:32
  274.8 7.1 %fusion.15 = f32[8192,512]{1,0:T(8,128)S(1)} fusion(bf16[8192,512]{1,0:T(8,128)(2,1)} %bitcast.5, bf16[512,512]{1,0:T(8,128)(2,1)S(1)} %copy-done), kind=kOutput, calls=%fused_computation.43 | convolution fusion | flops 4294967296 | bytes 25690112 | tf_op jit(solution)/shard_map/dot_general | solution.py:43
  281.9 1.6 fusion.3
  283.5 4.1 copy-done.1
  287.6 0.8 fusion.16
  288.5 42.6 %all-reduce.4.cloned.1.call-done = f32[128,256]{1,0:T(8,128)} async-done(((f32[128,256]{1,0:T(8,128)}), f32[128,256]{1,0:T(8,128)}) %all-reduce.4.cloned.1.call-update) | async-done | bytes 131088 | tf_op jit(solution)/shard_map/psum | solution.py:47
  331.1 1.0 exponential_reduce_fusion
  332.1 1.1 convolution_convert_fusion
  333.2 16.1 %fusion.2 = f32[512,512]{1,0:T(8,128)} fusion(bf16[8192,512]{1,0:T(8,128)(2,1)} %bitcast.5, f32[8192,512]{1,0:T(8,128)} %copy-done.1, bf16[128,8192]{1,0:T(8,128)(2,1)S(1)} %reshape.150, bf16[128,512]{1,0:T(8,128)(2,1)S(1)} %convolution_convert_fusion), kind=kOutput, calls=%fused_computation.7 | convolution fusion | flops 5381292032 | bytes 28442624 | tf_op jit(solution)/shard_map/dot_general | solution.py:64
  349.3 1.1 fusion.14
  350.5 189.7 %all-reduce.6.cloned.1.call-done = (f32[512,512]{1,0:T(8,128)}, f32[512,256]{1,0:T(8,128)}) async-done(((f32[512,512]{1,0:T(8,128)}, f32[512,256]{1,0:T(8,128)}), (f32[512,512]{1,0:T(8,128)}, f32[512,256]{1,0:T(8,128)})) %all-reduce.6.cloned.1.call-update) | async-done | bytes 1572880 | tf_op jit(solution)/shard_map/psum | solution.py:65
  540.2 2.3 copy.27
  542.4 1.9 copy.28
  (38 shorter events, 1.4 us)
Async XLA Ops:
  7.2 267.6 %copy-start = (bf16[512,512]{1,0:T(8,128)(2,1)S(1)}, bf16[512,512]{1,0:T(8,128)(2,1)}, u32[]{:S(2)}) copy-start(bf16[512,512]{1,0:T(8,128)(2,1)} %param.10) | copy-start | bytes 1572868
  82.8 6.0 %copy-start.4 = (bf16[128,32]{0,1:T(8,128)(2,1)S(1)}, bf16[128,32]{0,1:T(8,128)(2,1)}, u32[]{:S(2)}) copy-start(bf16[128,32]{0,1:T(8,128)(2,1)} %param.8) | copy-start | bytes 24580
  82.8 6.2 %copy-start.7 = (s32[2]{0:T(128)S(1)}, s32[2]{0:T(128)}, u32[]{:S(2)}) copy-start(s32[2]{0:T(128)} %constant.51) | copy-start | bytes 28
  82.8 6.3 %copy-start.6 = (s32[2]{0:T(128)S(1)}, s32[2]{0:T(128)}, u32[]{:S(2)}) copy-start(s32[2]{0:T(128)} %constant.54) | copy-start | bytes 28
  82.8 191.9 %all-to-all-start.1 = ((bf16[64,128,512]{2,1,0:T(8,128)(2,1)}), bf16[64,128,512]{2,1,0:T(8,128)(2,1)}, u32[]{:S(2)}, u32[]{:S(2)}) async-start(bf16[64,128,512]{2,1,0:T(8,128)(2,1)} %bitcast.21), calls=%async_computation.1 | async-start | bytes 16777216 | tf_op jit(solution)/shard_map/all_to_all | solution.py:32
  88.7 242.3 %all-reduce.4.cloned.1.call-start = ((), (), s32[]{:S(2)}) async-start(), calls=%async_computation.2 | async-start | bytes 262144 | tf_op jit(solution)/shard_map/psum | solution.py:47
  281.9 5.7 %copy-start.1 = (f32[8192,512]{1,0:T(8,128)}, f32[8192,512]{1,0:T(8,128)S(1)}, u32[]{:S(2)}) copy-start(f32[8192,512]{1,0:T(8,128)S(1)} %fusion.15) | copy-start | bytes 50331652
  281.9 5.7 %copy-start.3 = (bf16[512,256]{1,0:T(8,128)(2,1)S(1)}, bf16[512,256]{1,0:T(8,128)(2,1)}, u32[]{:S(2)}) copy-start(bf16[512,256]{1,0:T(8,128)(2,1)} %param.11) | copy-start | bytes 786436
  281.9 50.2 %copy-start.5 = (s32[128]{0:T(128)S(1)}, s32[128]{0:T(128)}, u32[]{:S(2)}) copy-start(s32[128]{0:T(128)} %param.9) | copy-start | bytes 1540
  288.5 251.7 %all-reduce.6.cloned.1.call-start = ((), (), s32[]{:S(2)}) async-start(), calls=%async_computation.3 | async-start | bytes 3145728 | tf_op jit(solution)/shard_map/psum | solution.py:65
  333.2 16.1 %copy-start.2 = (f32[128,256]{1,0:T(8,128)S(1)}, f32[128,256]{1,0:T(8,128)}, u32[]{:S(2)}) copy-start(f32[128,256]{1,0:T(8,128)} %all-reduce.4.cloned.1.call-done) | copy-start | bytes 393220
Sparse Core Ops, SparseCore 0:
  288.6 42.4 all-reduce.3
  350.6 189.5 all-reduce.5
where the time goes:
time: 552 us; the launch traced here: 551 us
  waiting for transfers between devices  385 us (70%)
  local copies, waits for them, and re-layouts  94.5 us (17%)
  matrix products  27.8 us (5%)
  blocking collectives  21.3 us (4%)
  between operations  14.3 us (3%)
  starting transfers between devices  5.97 us (1%)
    psum x1, waiting for transfers between devices, body(): grad_one, grad_two = lax.psum((grad_one, grad_two), ('own', 'col'))  190 us
    all_to_all x1, waiting for transfers between devices, body(): lax.all_to_all(fetched, ('own', 'col'), split_axis=0, concat_axis=0, tile...  152 us
    psum x1, waiting for transfers between devices, body(): logits = lax.psum(partial_logits, 'mlp')  42.6 us
    unnamed x20, local copies, waits for them, and re-layouts  38.8 us
    gather x1, local copies, waits for them, and re-layouts, body(): fetched = features[asked_rows]  36.5 us
    all_to_all x1, blocking collectives, body(): lax.all_to_all(requests, ('own', 'col'), split_axis=0, concat_axis=0, til...  21.3 us
    dot_general x1, matrix products, body(): lax.dot_general(received, d_pre, contract_first, preferred_element_type=j...  16.1 us
    scatter x1, local copies, waits for them, and re-layouts, body(): jnp.zeros((owners * capacity,), jnp.int32).at[flat_slot]  15.5 us
  transfers between devices with their start and end apart: 3, of which 3 were waited for; matrix products, arithmetic and copies ran while one was open for 6% of the time, Pallas kernels for 0%

commit v1 on v0

--- a/solution.py
+++ b/solution.py
@@ -44,7 +44,7 @@
     active = jnp.maximum(pre_act, 0.0).astype(jnp.bfloat16)
     hidden = jnp.dot(spread, active, preferred_element_type=jnp.float32).astype(jnp.bfloat16)
     partial_logits = jnp.dot(hidden, w_two, preferred_element_type=jnp.float32)
-    logits = lax.psum(partial_logits, "mlp")
+    logits = jnp.sum(lax.all_gather(partial_logits, "mlp"), axis=0)
     exponent = jnp.exp(logits)
     probability = exponent / jnp.sum(exponent, axis=1, keepdims=True)
     classes = w_two.shape[1]

time: 552 us -> 517 us (0.937)
  waiting for transfers between devices: 385 us -> 338 us
  blocking collectives: 21.3 us -> 34.4 us
    psum x1 -> x0, waiting for transfers between devices: 42.6 us -> none  [body(): logits = lax.psum(partial_logits, 'mlp')]
    all_gather x0 -> x1, blocking collectives: none -> 13.1 us  [body(): logits = jnp.sum(lax.all_gather(partial_logits, 'mlp'), axis=0)]
    unnamed x20 -> x18, local copies, waits for them, and re-layouts: 38.8 us -> 38.8 us
  transfers between devices with their start and end apart: 3 -> 2, of which waited for: 3 -> 2; matrix products, arithmetic and copies ran while one was open for 6% -> 7% of each run, Pallas kernels for 0% -> 0%
where the time goes in v1:
time: 517 us; the launch traced here: 516 us
  waiting for transfers between devices  338 us (65%)
  local copies, waits for them, and re-layouts  94.5 us (18%)
  blocking collectives  34.4 us (7%)
  matrix products  27.2 us (5%)
  between operations  14.3 us (3%)
  starting transfers between devices  5.93 us (1%)
    psum x1, waiting for transfers between devices, body(): grad_one, grad_two = lax.psum((grad_one, grad_two), ('own', 'col'))  186 us
    all_to_all x1, waiting for transfers between devices, body(): lax.all_to_all(fetched, ('own', 'col'), split_axis=0, concat_axis=0, tile...  152 us
    unnamed x18, local copies, waits for them, and re-layouts  38.8 us
    gather x1, local copies, waits for them, and re-layouts, body(): fetched = features[asked_rows]  36.5 us
    all_to_all x1, blocking collectives, body(): lax.all_to_all(requests, ('own', 'col'), split_axis=0, concat_axis=0, til...  21.3 us
    dot_general x1, matrix products, body(): lax.dot_general(received, d_pre, contract_first, preferred_element_type=j...  16.1 us
    scatter x1, local copies, waits for them, and re-layouts, body(): jnp.zeros((owners * capacity,), jnp.int32).at[flat_slot]  15.5 us
    all_gather x1, blocking collectives, body(): logits = jnp.sum(lax.all_gather(partial_logits, 'mlp'), axis=0)  13.1 us
  transfers between devices with their start and end apart: 2, of which 2 were waited for; matrix products, arithmetic and copies ran while one was open for 7% of the time, Pallas kernels for 0%

profile of v1, /device:TPU:8, one launch (start us, length us, event | category | flops | bytes accessed | tf_op | source)
XLA Modules:
  0.0 516.3 jit_solution(13794221402228512433)
XLA Ops:
  7.2 0.8 add_select_fusion
  8.0 0.1 convert_reduce_fusion
  8.6 0.2 reduce_window_sum.22
  8.8 0.2 select_reduce_fusion
  9.4 15.5 %scatter_custom_fusion = s32[8192]{0:T(1024)S(1)} fusion(s32[4096]{0:T(1024)S(1)} %bitcast.24, s32[4096]{0:T(1024)S(1)} %reshape.163, s32[]{:T(128)} %constant.41.clone.1), kind=kCustom, calls=%fused_computation.34 | custom fusion | bytes 32772 | tf_op jit(solution)/shard_map/scatter | solution.py:28
  25.0 21.3 %all_to_all.17 = s32[64,1,128]{2,1,0:T(1,128)S(1)} all-to-all(s32[64,1,128]{2,1,0:T(1,128)S(1)} %bitcast.25), channel_id=1, replica_groups=mesh['own'=8,'col'=8,'mlp'=4] {'own','col'}, dimensions={0} | all-to-all | bytes 65536 | tf_op jit(solution)/shard_map/all_to_all | solution.py:30
  46.3 36.5 %gather_fusion = bf16[8192,512]{1,0:T(8,128)(2,1)} fusion(bf16[4096,512]{1,0:T(8,128)(2,1)} %param.6, s32[8192]{0:T(1024)S(1)} %fusion.7), kind=kCustom, calls=%fused_computation | custom fusion | bytes 16809984 | tf_op jit(solution)/shard_map/gather | solution.py:31
  82.8 5.9 %all-to-all-start.1 = ((bf16[64,128,512]{2,1,0:T(8,128)(2,1)}), bf16[64,128,512]{2,1,0:T(8,128)(2,1)}, u32[]{:S(2)}, u32[]{:S(2)}) async-start(bf16[64,128,512]{2,1,0:T(8,128)(2,1)} %bitcast.22), calls=%async_computation.1 | async-start | bytes 16777216 | tf_op jit(solution)/shard_map/all_to_all | solution.py:32
  88.8 0.1 copy.23
  89.1 0.1 and_reduce_fusion
  89.3 30.4 %scatter_custom_fusion.1 = bf16[1048576]{0:T(1024)(128)(2,1)} fusion(s32[4096]{0:T(1024)S(1)} %broadcast_select_fusion, bf16[4096]{0:T(1024)(128)(2,1)S(1)} %reshape.169, bf16[]{:T(256)} %constant.50.clone.1), kind=kCustom, calls=%fused_computation.10 | custom fusion | bytes 2097154
  119.7 2.8 reshape.150
  122.5 152.3 %all-to-all-done.1 = bf16[64,128,512]{2,1,0:T(8,128)(2,1)} async-done(((bf16[64,128,512]{2,1,0:T(8,128)(2,1)}), bf16[64,128,512]{2,1,0:T(8,128)(2,1)}, u32[]{:S(2)}, u32[]{:S(2)}) %all-to-all-start.1) | async-done | bytes 8388640 | tf_op jit(solution)/shard_map/all_to_all | solution.py:32
  274.8 7.1 %fusion.15 = f32[8192,512]{1,0:T(8,128)S(1)} fusion(bf16[8192,512]{1,0:T(8,128)(2,1)} %bitcast.5, bf16[512,512]{1,0:T(8,128)(2,1)S(1)} %copy-done), kind=kOutput, calls=%fused_computation.43 | convolution fusion | flops 4294967296 | bytes 25690112 | tf_op jit(solution)/shard_map/dot_general | solution.py:43
  281.9 1.6 fusion.3
  283.5 4.1 copy-done.1
  287.6 0.2 fusion.16
  287.8 13.1 %all-gather = f32[512,256]{1,0:T(8,128)S(1)} all-gather(f32[128,256]{1,0:T(8,128)S(1)} %fusion.16), channel_id=2, replica_groups=mesh['own'=8,'col'=8,'mlp'=4] {'mlp'}, dimensions={0}, use_global_device_ids=true | all-gather | bytes 655360 | tf_op jit(solution)/shard_map/all_gather | solution.py:47
  301.0 1.2 convolution_convert_fusion
  302.2 1.1 fusion.14
  303.3 16.1 %fusion.2 = f32[512,512]{1,0:T(8,128)} fusion(bf16[8192,512]{1,0:T(8,128)(2,1)} %bitcast.5, f32[8192,512]{1,0:T(8,128)} %copy-done.1, bf16[128,8192]{1,0:T(8,128)(2,1)S(1)} %reshape.150, bf16[128,512]{1,0:T(8,128)(2,1)S(1)} %convolution_convert_fusion), kind=kOutput, calls=%fused_computation.7 | convolution fusion | flops 5381292032 | bytes 28442624 | tf_op jit(solution)/shard_map/dot_general | solution.py:64
  319.4 185.9 %all-reduce.3.cloned.1.call-done = (f32[512,512]{1,0:T(8,128)}, f32[512,256]{1,0:T(8,128)}) async-done(((f32[512,512]{1,0:T(8,128)}, f32[512,256]{1,0:T(8,128)}), (f32[512,512]{1,0:T(8,128)}, f32[512,256]{1,0:T(8,128)})) %all-reduce.3.cloned.1.call-update) | async-done | bytes 1572880 | tf_op jit(solution)/shard_map/psum | solution.py:65
  505.3 2.3 copy.26
  507.6 1.9 copy.27
  (35 shorter events, 1.3 us)
Async XLA Ops:
  7.2 267.6 %copy-start = (bf16[512,512]{1,0:T(8,128)(2,1)S(1)}, bf16[512,512]{1,0:T(8,128)(2,1)}, u32[]{:S(2)}) copy-start(bf16[512,512]{1,0:T(8,128)(2,1)} %param.10) | copy-start | bytes 1572868
  82.8 6.0 %copy-start.3 = (bf16[128,32]{0,1:T(8,128)(2,1)S(1)}, bf16[128,32]{0,1:T(8,128)(2,1)}, u32[]{:S(2)}) copy-start(bf16[128,32]{0,1:T(8,128)(2,1)} %param.8) | copy-start | bytes 24580
  82.8 6.2 %copy-start.6 = (s32[2]{0:T(128)S(1)}, s32[2]{0:T(128)}, u32[]{:S(2)}) copy-start(s32[2]{0:T(128)} %constant.51) | copy-start | bytes 28
  82.8 6.3 %copy-start.5 = (s32[2]{0:T(128)S(1)}, s32[2]{0:T(128)}, u32[]{:S(2)}) copy-start(s32[2]{0:T(128)} %constant.54) | copy-start | bytes 28
  82.8 191.9 %all-to-all-start.1 = ((bf16[64,128,512]{2,1,0:T(8,128)(2,1)}), bf16[64,128,512]{2,1,0:T(8,128)(2,1)}, u32[]{:S(2)}, u32[]{:S(2)}) async-start(bf16[64,128,512]{2,1,0:T(8,128)(2,1)} %bitcast.22), calls=%async_computation.1 | async-start | bytes 16777216 | tf_op jit(solution)/shard_map/all_to_all | solution.py:32
  88.7 416.6 %all-reduce.3.cloned.1.call-start = ((), (), s32[]{:S(2)}) async-start(), calls=%async_computation.2 | async-start | bytes 3145728 | tf_op jit(solution)/shard_map/psum | solution.py:65
  281.9 5.7 %copy-start.1 = (f32[8192,512]{1,0:T(8,128)}, f32[8192,512]{1,0:T(8,128)S(1)}, u32[]{:S(2)}) copy-start(f32[8192,512]{1,0:T(8,128)S(1)} %fusion.15) | copy-start | bytes 50331652
  281.9 5.7 %copy-start.2 = (bf16[512,256]{1,0:T(8,128)(2,1)S(1)}, bf16[512,256]{1,0:T(8,128)(2,1)}, u32[]{:S(2)}) copy-start(bf16[512,256]{1,0:T(8,128)(2,1)} %param.11) | copy-start | bytes 786436
  281.9 19.1 %copy-start.4 = (s32[128]{0:T(128)S(1)}, s32[128]{0:T(128)}, u32[]{:S(2)}) copy-start(s32[128]{0:T(128)} %param.9) | copy-start | bytes 1540
Sparse Core Ops, SparseCore 0:
  319.5 185.7 all-reduce.2
